TPU v7x, 32 devices: a whole 2x2x4 slice. The times are simulated.
32 devices in a mesh: layer: 8 (over z, x), tok: 4 (over y, core).
Axes of the slice: x: 2, y: 2, z: 4, core: 2. Of those that a mesh axis runs over, the one named last changes fastest.
Arguments:
- acts: bfloat16 [8, 128, 2048], P('layer', 'tok'), may hold values from -6 to 6
- w_enc: bfloat16 [8, 2048, 1024], P('layer', 'tok'), may hold values from -0.125 to 0.125
- b_enc: float32 [8, 1024], P('layer'), may hold values from -0.5 to 0.5
- w_dec: bfloat16 [8, 8, 1024, 2048], P('layer', None, None, 'tok'), may hold values from -0.0625 to 0.0625
- targets: bfloat16 [8, 128, 2048], P('layer', None, 'tok'), may hold values from -6 to 6
Outputs:
- code_grad: float32 [8, 128, 1024], P('layer', 'tok')
- dec_grad: bfloat16 [8, 8, 1024, 2048], P('layer', None, None, 'tok')
All inputs are finite; a program needn't handle non-finite values.
Results may differ from a plain program's by a relative error of at most 0.0034.
Values may be sent and summed in bfloat16 or wider, within the bound.
A program may use at most 64 MiB of HBM per device.

v0:
```python
import functools

import jax
import jax.numpy as jnp
from jax import lax
from jax.experimental import pallas as pl
from jax.experimental.pallas import tpu as pltpu
from jax.sharding import PartitionSpec as P

MESH = pl.DeviceIdType.MESH
BF = jnp.bfloat16
F32 = jnp.float32


def exchange(
    n, t, acts, w_enc, bias, w_dec, targets,
    codes, errs, grads,
    acts_v, wenc_v, wdec_v, pre, pre_in, pair_out, pair_in, codes_v,
    held, mix_out, mix_in, fwd_out, fwd_in, bwd_out, bwd_in, err_v,
    cg, cg_in, cg_out, cg_far,
    s_wenc, s_wdec, s_acts, a_send, a_recv, p_sem, y_send, y_recv, c_sem,
    m_send, m_recv, f_send, f_recv, b_send, b_recv, e_send, e_recv, g_sem, gy_send, gy_recv,
):
    groups, chips = n // 2, t // 2
    i, k = lax.axis_index("layer"), lax.axis_index("tok")
    g, p = i // 2, i % 2
    y, c = k // 2, k % 2
    other_layer = 2 * g + 1 - p
    other_core = 2 * y + 1 - c
    rows, depth = acts.shape[1], wenc_v.shape[0]
    features, width = wdec_v.shape[1], wdec_v.shape[2]
    half_f, half_w = features // 2, width // 2
    tokens = rows * t
    first = 2 * g
    count = n - first

    def remote(src, dst, send, recv, layer, tok):
        return pltpu.make_async_remote_copy(
            src_ref=src, dst_ref=dst, send_sem=send, recv_sem=recv,
            device_id=(layer, tok), device_id_type=MESH,
        )

    wenc_copy = pltpu.make_async_copy(w_enc.at[0], wenc_v, s_wenc)
    wenc_copy.start()
    own_cols = pl.ds(pl.multiple_of(k * depth, depth), depth)
    own_rows = pl.ds(pl.multiple_of(k * rows, rows), rows)
    acts_copy = pltpu.make_async_copy(acts.at[0, :, own_cols], acts_v.at[own_rows, :], s_acts)
    acts_copy.start()

    def dec_copy(j):
        return pltpu.make_async_copy(w_dec.at[0, j], wdec_v.at[j], s_wdec.at[j])

    barrier = pltpu.get_barrier_semaphore()
    for step in range(1, t):
        pl.semaphore_signal(
            barrier, inc=1, device_id=(i, lax.rem(k + step, t)), device_id_type=MESH
        )
    pl.semaphore_signal(barrier, inc=1, device_id=(other_layer, k), device_id_type=MESH)

    @pl.when(g > 0)
    def _():
        pl.semaphore_signal(barrier, inc=1, device_id=(i - 2, k), device_id_type=MESH)

    @pl.when(g < groups - 1)
    def _():
        pl.semaphore_signal(barrier, inc=1, device_id=(i + 2, k), device_id_type=MESH)

    @pl.when(g == 0)
    def _():
        fwd_in[...] = jnp.zeros_like(fwd_in)

    for q in range(2):
        bwd_in[first + q] = jnp.zeros(bwd_in.shape[1:], BF)

    linked = (g > 0).astype(jnp.int32) + (g < groups - 1).astype(jnp.int32)
    pl.semaphore_wait(barrier, t + linked)

    def acts_send(peer):
        cols = pl.ds(pl.multiple_of(peer * depth, depth), depth)
        return remote(
            acts.at[0, :, cols], acts_v.at[own_rows, :], a_send.at[peer], a_recv.at[k], i, peer
        )

    def acts_land(peer):
        lines = pl.ds(pl.multiple_of(peer * rows, rows), rows)
        return remote(
            acts.at[0, :, own_cols], acts_v.at[lines, :], a_send.at[peer], a_recv.at[peer], i, peer
        )

    for step in range(1, t):
        acts_send(lax.rem(k + step, t)).start()

    def start_dec(q, _):
        dec_copy(n - 1 - q).start()
        return 0

    lax.fori_loop(0, count, start_dec, 0)
    wenc_copy.wait()
    acts_copy.wait()
    for step in range(1, t):
        acts_land(lax.rem(k + step, t)).wait_recv()

    for h in range(2):
        pre[h] = jnp.dot(
            acts_v[...], wenc_v[:, h * half_f:(h + 1) * half_f], preferred_element_type=F32
        )
    pre_copy = remote(pre.at[1 - c], pre_in, p_sem.at[0], p_sem.at[1], i, other_core)
    pre_copy.start()
    pre_copy.wait_recv()
    chip_sum = pre[c] + pre_in[...]
    pair_out[...] = chip_sum.astype(BF)

    def pair_send(peer):
        return remote(pair_out, pair_in.at[y], y_send.at[peer], y_recv.at[y], i, 2 * peer + c)

    def pair_land(peer):
        return remote(pair_out, pair_in.at[peer], y_send.at[peer], y_recv.at[peer], i, 2 * peer + c)

    for step in range(1, chips):
        pair_send(lax.rem(y + step, chips)).start()
    pre_in[...] = chip_sum + bias[pl.ds(c, 1), :]
    for step in range(1, chips):
        peer = lax.rem(y + step, chips)
        pair_land(peer).wait_recv()
        pre_in[...] += pair_in[peer].astype(F32)
    codes_v[c] = jnp.maximum(pre_in[...], 0.0).astype(BF)
    codes_copy = remote(codes_v.at[c], codes_v.at[c], c_sem.at[0], c_sem.at[1], i, other_core)
    codes_copy.start()
    codes_land = remote(
        codes_v.at[c], codes_v.at[1 - c], c_sem.at[0], c_sem.at[1], i, other_core
    )
    codes_land.wait_recv()
    codes[...] = codes_v[...]

    def mix(j):
        return remote(mix_out.at[j], mix_in.at[j], m_send.at[j], m_recv.at[j], other_layer, k)

    def ahead(j):
        return remote(fwd_out.at[j], fwd_in.at[j], f_send.at[j], f_recv.at[j], i + 2, k)

    def back(j):
        return remote(bwd_out.at[j], bwd_in.at[j], b_send.at[j], b_recv.at[j], i - 2, k)

    def share(j):
        return remote(err_v.at[j, p], err_v.at[j, p], e_send.at[j], e_recv.at[j], other_layer, k)

    def share_land(j):
        return remote(
            err_v.at[j, p], err_v.at[j, 1 - p], e_send.at[j], e_recv.at[j], other_layer, k
        )

    def decode(q, _):
        j = n - 1 - q
        dec_copy(j).wait()
        both = []
        for h in range(2):
            cols = slice(h * half_w, (h + 1) * half_w)
            product = jnp.dot(
                codes_v[0], wdec_v[j, :half_f, cols], preferred_element_type=F32
            ) + jnp.dot(codes_v[1], wdec_v[j, half_f:, cols], preferred_element_type=F32)
            product = jnp.where(j >= i, product, 0.0)
            goal = targets[0, :, cols].astype(F32)
            both.append(product - jnp.where(j == i, goal, 0.0))
        held[j] = jnp.where(p == 0, both[0], both[1])
        mix_out[j] = jnp.where(p == 0, both[1], both[0]).astype(BF)
        mix(j).start()
        return 0

    lax.fori_loop(0, count, decode, 0)

    def gather_pair(j):
        mix(j).wait_recv()
        held[j] = held[j] + mix_in[j].astype(F32)

    def wait_ahead(j):
        @pl.when(g > 0)
        def _():
            ahead(j).wait_recv()

    def wait_back(j):
        @pl.when(j >= first + 2)
        def _():
            back(j).wait_recv()

    def send_ahead(j):
        @pl.when(j >= first + 2)
        def _():
            fwd_out[j] = (held[j] + fwd_in[j].astype(F32)).astype(BF)
            ahead(j).start()

    def send_back(j):
        @pl.when(g > 0)
        def _():
            bwd_out[j] = (held[j] + bwd_in[j].astype(F32)).astype(BF)
            back(j).start()

    def finish(j):
        total = held[j] + fwd_in[j].astype(F32) + bwd_in[j].astype(F32)
        err_v[j, p] = total.astype(BF)
        share(j).start()

    @pl.when(g < groups // 2)
    def _():
        def one(q, _):
            j = n - 1 - q
            gather_pair(j)
            wait_ahead(j)
            send_ahead(j)
            return 0

        def two(q, _):
            j = n - 1 - q
            wait_back(j)
            send_back(j)
            finish(j)
            return 0

        lax.fori_loop(0, count, one, 0)
        lax.fori_loop(0, count, two, 0)

    @pl.when(g >= groups // 2)
    def _():
        def one(q, _):
            j = n - 1 - q
            gather_pair(j)
            wait_back(j)
            send_back(j)
            return 0

        def two(q, _):
            j = n - 1 - q
            wait_ahead(j)
            send_ahead(j)
            finish(j)
            return 0

        lax.fori_loop(0, count, one, 0)
        lax.fori_loop(0, count, two, 0)

    cg[...] = jnp.zeros_like(cg)

    def backward(q, _):
        j = n - 1 - q
        share_land(j).wait_recv()
        keep = j >= i
        errs[j] = jnp.where(keep, err_v[j], jnp.zeros_like(err_v[j]))

        @pl.when(keep)
        def _():
            nt = (((1,), (1,)), ((), ()))
            part = lax.dot_general(
                err_v[j, 0], wdec_v[j, :, :half_w], nt, preferred_element_type=F32
            ) + lax.dot_general(
                err_v[j, 1], wdec_v[j, :, half_w:], nt, preferred_element_type=F32
            )
            cg[...] += part.reshape(cg.shape)

        return 0

    lax.fori_loop(0, count, backward, 0)

    def blank(j, _):
        errs[j] = jnp.zeros(errs.shape[1:], BF)
        return 0

    lax.fori_loop(0, first, blank, 0)

    cg_copy = remote(cg.at[:, 1 - c], cg_in, g_sem.at[0], g_sem.at[1], i, other_core)
    cg_copy.start()
    cg_copy.wait_recv()

    def far_send(peer):
        return remote(
            cg_out.at[peer], cg_far.at[y], gy_send.at[peer], gy_recv.at[y], i, 2 * peer + c
        )

    def far_land(peer):
        return remote(
            cg_out.at[peer], cg_far.at[peer], gy_send.at[peer], gy_recv.at[peer], i, 2 * peer + c
        )

    for step in range(1, chips):
        peer = lax.rem(y + step, chips)
        cg_out[peer] = (cg[peer, c] + cg_in[peer]).astype(BF)
        far_send(peer).start()
    grads[...] = cg[y, c] + cg_in[y]
    for step in range(1, chips):
        peer = lax.rem(y + step, chips)
        far_land(peer).wait_recv()
        grads[...] += cg_far[peer].astype(F32)

    for step in range(1, t):
        acts_send(lax.rem(k + step, t)).wait_send()
    pre_copy.wait_send()
    codes_copy.wait_send()
    cg_copy.wait_send()
    for step in range(1, chips):
        peer = lax.rem(y + step, chips)
        pair_send(peer).wait_send()
        far_send(peer).wait_send()

    def drain(q, _):
        j = n - 1 - q
        mix(j).wait_send()
        share(j).wait_send()

        @pl.when(j >= first + 2)
        def _():
            ahead(j).wait_send()

        @pl.when(g > 0)
        def _():
            back(j).wait_send()

        return 0

    lax.fori_loop(0, count, drain, 0)


def weight_grads(codes, errs, grads_in, dec, grads):
    grads[...] = grads_in[...]
    tn = (((0,), (0,)), ((), ()))
    half_f, half_w = codes.shape[2], errs.shape[3]
    for a in range(2):
        for b in range(2):
            dec[0, 0, a * half_f:(a + 1) * half_f, b * half_w:(b + 1) * half_w] = lax.dot_general(
                codes[a], errs[0, b], tn, preferred_element_type=F32
            ).astype(BF)


def local(acts, w_enc, b_enc, w_dec, targets):
    n, t = lax.axis_size("layer"), lax.axis_size("tok")
    _, rows, model = acts.shape
    _, depth, features = w_enc.shape
    width = w_dec.shape[3]
    tokens = rows * t
    half_f, half_w = features // 2, width // 2
    chips = t // 2
    vmem = pl.BlockSpec(memory_space=pltpu.VMEM)
    hbm = pl.BlockSpec(memory_space=pl.ANY)
    block = (n, tokens, half_w)
    dma = pltpu.SemaphoreType.DMA
    codes, errs, grads = pl.pallas_call(
        functools.partial(exchange, n, t),
        out_shape=(
            jax.ShapeDtypeStruct((2, tokens, half_f), BF),
            jax.ShapeDtypeStruct((n, 2, tokens, half_w), BF),
            jax.ShapeDtypeStruct((rows, features), F32),
        ),
        in_specs=[hbm, hbm, vmem, hbm, vmem],
        out_specs=(vmem, vmem, vmem),
        scratch_shapes=[
            pltpu.VMEM((tokens, depth), BF),
            pltpu.VMEM((depth, features), BF),
            pltpu.VMEM((n, features, width), BF),
            pltpu.VMEM((2, tokens, half_f), F32),
            pltpu.VMEM((tokens, half_f), F32),
            pltpu.VMEM((tokens, half_f), BF),
            pltpu.VMEM((chips, tokens, half_f), BF),
            pltpu.VMEM((2, tokens, half_f), BF),
            pltpu.VMEM(block, F32),
            pltpu.VMEM(block, BF),
            pltpu.VMEM(block, BF),
            pltpu.VMEM(block, BF),
            pltpu.VMEM(block, BF),
            pltpu.VMEM(block, BF),
            pltpu.VMEM(block, BF),
            pltpu.VMEM((n, 2, tokens, half_w), BF),
            pltpu.VMEM((chips, 2, rows, features), F32),
            pltpu.VMEM((chips, rows, features), F32),
            pltpu.VMEM((chips, rows, features), BF),
            pltpu.VMEM((chips, rows, features), BF),
            dma, dma((n,)), dma, dma((t,)), dma((t,)), dma((2,)),
            dma((chips,)), dma((chips,)), dma((2,)),
            dma((n,)), dma((n,)), dma((n,)), dma((n,)), dma((n,)), dma((n,)),
            dma((n,)), dma((n,)), dma((2,)), dma((chips,)), dma((chips,)),
        ],
        compiler_params=pltpu.CompilerParams(
            collective_id=0, has_side_effects=True, vmem_limit_bytes=56 * 2**20
        ),
        name="exchange",
    )(acts, w_enc, b_enc.reshape(2, half_f), w_dec, targets)
    dec, code_share = pl.pallas_call(
        weight_grads,
        grid=(n,),
        out_shape=(
            jax.ShapeDtypeStruct((1, n, features, width), BF),
            jax.ShapeDtypeStruct((rows, features), F32),
        ),
        in_specs=[
            pl.BlockSpec((2, tokens, half_f), lambda j: (0, 0, 0)),
            pl.BlockSpec((1, 2, tokens, half_w), lambda j: (j, 0, 0, 0)),
            pl.BlockSpec((rows, features), lambda j: (0, 0)),
        ],
        out_specs=(
            pl.BlockSpec((1, 1, features, width), lambda j: (0, j, 0, 0)),
            pl.BlockSpec((rows, features), lambda j: (0, 0)),
        ),
        compiler_params=pltpu.CompilerParams(vmem_limit_bytes=40 * 2**20),
        name="weight_grads",
    )(codes, errs, grads)
    return (code_share[None], dec)


def solution(mesh):
    return jax.shard_map(
        local,
        mesh=mesh,
        in_specs=(
            P("layer", "tok", None),
            P("layer", "tok", None),
            P("layer", None),
            P("layer", None, None, "tok"),
            P("layer", None, "tok"),
        ),
        out_specs=(P("layer", "tok", None), P("layer", None, None, "tok")),
        check_vma=False,
    )
```

profile of v0, /device:TPU:1, one launch (start us, length us, event | category | flops | bytes accessed | tf_op | source)
XLA Modules:
  0.0 64.2 jit_solution(2165554183040200869)
XLA Ops:
  0.6 0.5 broadcast.3
  1.1 1.3 %reduce.3 = f32[1024]{0:T(1024)S(1)} reduce(f32[1,1024]{1,0:T(1,128)} %param.7, f32[]{:T(128)} %broadcast.3), dimensions={0}, to_apply=%param.7.reduce_sub_computation.3 | reduce | bytes 8196 | tf_op args[2]
  2.5 0.6 reshape.7.bias
  3.1 51.8 %exchange.1 = (bf16[2,128,512]{2,1,0:T(8,128)(2,1)}, bf16[8,2,128,256]{3,2,1,0:T(8,128)(2,1)}, f32[32,1024]{1,0:T(8,128)}) custom-call(bf16[1,32,2048]{2,1,0:T(8,128)(2,1)} %acts.1, bf16[1,512,1024]{2,1,0:T(8,128)(2,1)} %w_enc.1, f32[2,512]{1,0:T(2,128)} %reshape.7.bias, bf16[1,8,1024,512]{3,2,1,0:T(8,128)(2,1)} %w_dec.1, bf16[1,128,512]{2,1,0:T(8,128)(2,1)} %targets.1), custom_call_target="tpu_custom_call" | custom-call | tf_op jit(solution)/shard_map/exchange/pallas_call | solution.py:343
  54.9 0.0 copy-start
  54.9 1.2 %copy-done = bf16[8,2,128,256]{3,2,1,0:T(8,128)(2,1)S(1)} copy-done((bf16[8,2,128,256]{3,2,1,0:T(8,128)(2,1)S(1)}, bf16[8,2,128,256]{3,2,1,0:T(8,128)(2,1)}, u32[]{:S(2)}) %copy-start) | copy-done | bytes 1048600
  56.2 0.0 copy-start.1
  56.2 0.9 %copy-done.1 = bf16[2,128,512]{2,1,0:T(8,128)(2,1)S(1)} copy-done((bf16[2,128,512]{2,1,0:T(8,128)(2,1)S(1)}, bf16[2,128,512]{2,1,0:T(8,128)(2,1)}, u32[]{:S(2)}) %copy-start.1) | copy-done | bytes 262168
  57.1 0.0 copy-start.2
  57.1 0.9 %copy-done.2 = f32[32,1024]{1,0:T(8,128)S(1)} copy-done((f32[32,1024]{1,0:T(8,128)S(1)}, f32[32,1024]{1,0:T(8,128)}, u32[]{:S(2)}) %copy-start.2) | copy-done | bytes 131096
  58.0 6.2 %weight_grads.1 = (bf16[1,8,1024,512]{3,2,1,0:T(8,128)(2,1)}, f32[32,1024]{1,0:T(8,128)}) custom-call(bf16[2,128,512]{2,1,0:T(8,128)(2,1)S(1)} %copy-done.1, bf16[8,2,128,256]{3,2,1,0:T(8,128)(2,1)S(1)} %copy-done, f32[32,1024]{1,0:T(8,128)S(1)} %copy-done.2), custom_call_target="tpu_custom_call" | custom-call | tf_op jit(solution)/shard_map/weight_grads/pallas_call | solution.py:383
Async XLA Ops:
  54.9 1.2 %copy-start = (bf16[8,2,128,256]{3,2,1,0:T(8,128)(2,1)S(1)}, bf16[8,2,128,256]{3,2,1,0:T(8,128)(2,1)}, u32[]{:S(2)}) copy-start(bf16[8,2,128,256]{3,2,1,0:T(8,128)(2,1)} %get-tuple-element.8.errs) | copy-start | bytes 3145732
  56.2 0.9 %copy-start.1 = (bf16[2,128,512]{2,1,0:T(8,128)(2,1)S(1)}, bf16[2,128,512]{2,1,0:T(8,128)(2,1)}, u32[]{:S(2)}) copy-start(bf16[2,128,512]{2,1,0:T(8,128)(2,1)} %get-tuple-element.7.codes) | copy-start | bytes 786436
  57.1 0.9 %copy-start.2 = (f32[32,1024]{1,0:T(8,128)S(1)}, f32[32,1024]{1,0:T(8,128)}, u32[]{:S(2)}) copy-start(f32[32,1024]{1,0:T(8,128)} %get-tuple-element.9.grads_in) | copy-start | bytes 393220
where the time goes:
time: 64.5 us; the launch traced here: 64.2 us
  Pallas kernels  58 us (90%)
  local copies, waits for them, and re-layouts  4.18 us (6%)
  other arithmetic  1.35 us (2%)
  between operations  0.65 us (1%)
    pallas_call x1, Pallas kernels, local(): pl.pallas_call(functools.partial(exchange, n, t), out_shape=(jax.ShapeDty...  51.8 us
    pallas_call x1, Pallas kernels, local(): pl.pallas_call(weight_grads, grid=(n,), out_shape=(jax.ShapeDtypeStruct((...  6.2 us
    unnamed x7, local copies, waits for them, and re-layouts  3.58 us
    unnamed x1, other arithmetic  1.35 us

commit v1 on v0

--- a/solution.py
+++ b/solution.py
@@ -19,7 +19,7 @@
     held, mix_out, mix_in, fwd_out, fwd_in, bwd_out, bwd_in, err_v,
     cg, cg_in, cg_out, cg_far,
     s_wenc, s_wdec, s_acts, a_send, a_recv, p_sem, y_send, y_recv, c_sem,
-    m_send, m_recv, f_send, f_recv, b_send, b_recv, e_send, e_recv, g_sem, gy_send, gy_recv,
+    m_send, m_recv, f_send, f_recv, b_send, b_recv, e_send, e_recv, d_send, d_recv, g_sem, gy_send, gy_recv,
 ):
     groups, chips = n // 2, t // 2
     i, k = lax.axis_index("layer"), lax.axis_index("tok")
@@ -33,6 +33,7 @@
     tokens = rows * t
     first = 2 * g
     count = n - first
+    whole = n - max(0, min(n // 2, n - 4))
 
     def remote(src, dst, send, recv, layer, tok):
         return pltpu.make_async_remote_copy(
@@ -110,6 +111,8 @@
     chip_sum = pre[c] + pre_in[...]
     pair_out[...] = chip_sum.astype(BF)
 
+    own_half = pl.ds(pl.multiple_of(c * half_f, half_f), half_f)
+
     def pair_send(peer):
         return remote(pair_out, pair_in.at[y], y_send.at[peer], y_recv.at[y], i, 2 * peer + c)
 
@@ -118,7 +121,7 @@
 
     for step in range(1, chips):
         pair_send(lax.rem(y + step, chips)).start()
-    pre_in[...] = chip_sum + bias[pl.ds(c, 1), :]
+    pre_in[...] = chip_sum + bias[:, own_half]
     for step in range(1, chips):
         peer = lax.rem(y + step, chips)
         pair_land(peer).wait_recv()
@@ -130,7 +133,6 @@
         codes_v.at[c], codes_v.at[1 - c], c_sem.at[0], c_sem.at[1], i, other_core
     )
     codes_land.wait_recv()
-    codes[...] = codes_v[...]
 
     def mix(j):
         return remote(mix_out.at[j], mix_in.at[j], m_send.at[j], m_recv.at[j], other_layer, k)
@@ -148,6 +150,21 @@
         return remote(
             err_v.at[j, p], err_v.at[j, 1 - p], e_send.at[j], e_recv.at[j], other_layer, k
         )
+
+    def direct(j):
+        return remote(err_v.at[j], err_v.at[j], d_send.at[j], d_recv.at[j], i - 2, k)
+
+    def mix_leaves(j):
+        return (j > first) | ((p == 0) & (g > 0))
+
+    def mix_lands(j):
+        return (j > first) | ((p == 1) & (g > 0))
+
+    def share_leaves(j):
+        return ((j > first) | ((p == 1) & (g > 0))) & ((g > 0) | (j < whole))
+
+    def share_lands(j):
+        return ((j > first) | ((p == 0) & (g > 0))) & ((g > 0) | (j < whole))
 
     def decode(q, _):
         j = n - 1 - q
@@ -163,14 +180,27 @@
             both.append(product - jnp.where(j == i, goal, 0.0))
         held[j] = jnp.where(p == 0, both[0], both[1])
         mix_out[j] = jnp.where(p == 0, both[1], both[0]).astype(BF)
-        mix(j).start()
+
+        @pl.when(mix_leaves(j))
+        def _():
+            mix(j).start()
+
+        @pl.when((g == 0) & (j == first) & (p == 0))
+        def _():
+            err_v[j, 1] = mix_out[j]
+
         return 0
 
     lax.fori_loop(0, count, decode, 0)
+    for h in range(2):
+        codes[h] = codes_v[h].T
+    cg[...] = jnp.zeros_like(cg)
 
     def gather_pair(j):
-        mix(j).wait_recv()
-        held[j] = held[j] + mix_in[j].astype(F32)
+        @pl.when(mix_lands(j))
+        def _():
+            mix(j).wait_recv()
+            held[j] = held[j] + mix_in[j].astype(F32)
 
     def wait_ahead(j):
         @pl.when(g > 0)
@@ -189,7 +219,7 @@
             ahead(j).start()
 
     def send_back(j):
-        @pl.when(g > 0)
+        @pl.when((g > 1) | ((g == 1) & (j < whole)))
         def _():
             bwd_out[j] = (held[j] + bwd_in[j].astype(F32)).astype(BF)
             back(j).start()
@@ -197,28 +227,65 @@
     def finish(j):
         total = held[j] + fwd_in[j].astype(F32) + bwd_in[j].astype(F32)
         err_v[j, p] = total.astype(BF)
-        share(j).start()
-
-    @pl.when(g < groups // 2)
+
+        @pl.when(share_leaves(j))
+        def _():
+            share(j).start()
+
+    def arrive(j):
+        @pl.when(share_lands(j))
+        def _():
+            share_land(j).wait_recv()
+
+        @pl.when((g == 0) & (j >= whole))
+        def _():
+            direct(j).wait_recv()
+
+        @pl.when((g == 1) & (j >= whole))
+        def _():
+            direct(j).start()
+
+    early = (g > 0) & (g < groups // 2)
+
+    @pl.when(g == 0)
     def _():
         def one(q, _):
             j = n - 1 - q
             gather_pair(j)
-            wait_ahead(j)
             send_ahead(j)
             return 0
 
         def two(q, _):
-            j = n - 1 - q
+            j = whole - 1 - q
             wait_back(j)
-            send_back(j)
             finish(j)
             return 0
 
-        lax.fori_loop(0, count, one, 0)
-        lax.fori_loop(0, count, two, 0)
-
-    @pl.when(g >= groups // 2)
+        lax.fori_loop(0, n, one, 0)
+        lax.fori_loop(0, whole, two, 0)
+
+    @pl.when(early)
+    def _():
+        def one(q, _):
+            @pl.when(q < count)
+            def _():
+                j = n - 1 - q
+                gather_pair(j)
+                wait_ahead(j)
+                send_ahead(j)
+                wait_back(j)
+                send_back(j)
+                finish(j)
+
+            @pl.when(q >= 2)
+            def _():
+                arrive(n + 1 - q)
+
+            return 0
+
+        lax.fori_loop(0, count + 2, one, 0)
+
+    @pl.when((g > 0) & (g >= groups // 2))
     def _():
         def one(q, _):
             j = n - 1 - q
@@ -237,16 +304,21 @@
         lax.fori_loop(0, count, one, 0)
         lax.fori_loop(0, count, two, 0)
 
-    cg[...] = jnp.zeros_like(cg)
-
     def backward(q, _):
         j = n - 1 - q
-        share_land(j).wait_recv()
         keep = j >= i
-        errs[j] = jnp.where(keep, err_v[j], jnp.zeros_like(err_v[j]))
+
+        @pl.when(jnp.logical_not(early))
+        def _():
+            arrive(j)
+
+        @pl.when(jnp.logical_not(keep))
+        def _():
+            errs[j] = jnp.zeros(errs.shape[1:], BF)
 
         @pl.when(keep)
         def _():
+            errs[j] = err_v[j]
             nt = (((1,), (1,)), ((), ()))
             part = lax.dot_general(
                 err_v[j, 0], wdec_v[j, :, :half_w], nt, preferred_element_type=F32
@@ -301,14 +373,24 @@
 
     def drain(q, _):
         j = n - 1 - q
-        mix(j).wait_send()
-        share(j).wait_send()
+
+        @pl.when(mix_leaves(j))
+        def _():
+            mix(j).wait_send()
+
+        @pl.when(share_leaves(j))
+        def _():
+            share(j).wait_send()
+
+        @pl.when((g == 1) & (j >= whole))
+        def _():
+            direct(j).wait_send()
 
         @pl.when(j >= first + 2)
         def _():
             ahead(j).wait_send()
 
-        @pl.when(g > 0)
+        @pl.when((g > 1) | ((g == 1) & (j < whole)))
         def _():
             back(j).wait_send()
 
@@ -319,12 +401,11 @@
 
 def weight_grads(codes, errs, grads_in, dec, grads):
     grads[...] = grads_in[...]
-    tn = (((0,), (0,)), ((), ()))
-    half_f, half_w = codes.shape[2], errs.shape[3]
+    half_f, half_w = codes.shape[1], errs.shape[3]
     for a in range(2):
         for b in range(2):
-            dec[0, 0, a * half_f:(a + 1) * half_f, b * half_w:(b + 1) * half_w] = lax.dot_general(
-                codes[a], errs[0, b], tn, preferred_element_type=F32
+            dec[0, 0, a * half_f:(a + 1) * half_f, b * half_w:(b + 1) * half_w] = jnp.dot(
+                codes[a], errs[0, b], preferred_element_type=F32
             ).astype(BF)
 
 
@@ -343,7 +424,7 @@
     codes, errs, grads = pl.pallas_call(
         functools.partial(exchange, n, t),
         out_shape=(
-            jax.ShapeDtypeStruct((2, tokens, half_f), BF),
+            jax.ShapeDtypeStruct((2, half_f, tokens), BF),
             jax.ShapeDtypeStruct((n, 2, tokens, half_w), BF),
             jax.ShapeDtypeStruct((rows, features), F32),
         ),
@@ -373,13 +454,13 @@
             dma, dma((n,)), dma, dma((t,)), dma((t,)), dma((2,)),
             dma((chips,)), dma((chips,)), dma((2,)),
             dma((n,)), dma((n,)), dma((n,)), dma((n,)), dma((n,)), dma((n,)),
-            dma((n,)), dma((n,)), dma((2,)), dma((chips,)), dma((chips,)),
+            dma((n,)), dma((n,)), dma((n,)), dma((n,)), dma((2,)), dma((chips,)), dma((chips,)),
         ],
         compiler_params=pltpu.CompilerParams(
             collective_id=0, has_side_effects=True, vmem_limit_bytes=56 * 2**20
         ),
         name="exchange",
-    )(acts, w_enc, b_enc.reshape(2, half_f), w_dec, targets)
+    )(acts, w_enc, b_enc, w_dec, targets)
     dec, code_share = pl.pallas_call(
         weight_grads,
         grid=(n,),
@@ -388,7 +469,7 @@
             jax.ShapeDtypeStruct((rows, features), F32),
         ),
         in_specs=[
-            pl.BlockSpec((2, tokens, half_f), lambda j: (0, 0, 0)),
+            pl.BlockSpec((2, half_f, tokens), lambda j: (0, 0, 0)),
             pl.BlockSpec((1, 2, tokens, half_w), lambda j: (j, 0, 0, 0)),
             pl.BlockSpec((rows, features), lambda j: (0, 0)),
         ],
@@ -396,7 +477,7 @@
             pl.BlockSpec((1, 1, features, width), lambda j: (0, j, 0, 0)),
             pl.BlockSpec((rows, features), lambda j: (0, 0)),
         ),
-        compiler_params=pltpu.CompilerParams(vmem_limit_bytes=40 * 2**20),
+        compiler_params=pltpu.CompilerParams(vmem_limit_bytes=58 * 2**20),
         name="weight_grads",
     )(codes, errs, grads)
     return (code_share[None], dec)

time: 64.5 us -> 63.7 us (0.988)
  Pallas kernels: 58 us -> 62.8 us
  local copies, waits for them, and re-layouts: 4.18 us -> 0 us
  other arithmetic: 1.35 us -> 0 us
    unnamed x7 -> x0, local copies, waits for them, and re-layouts: 3.58 us -> none
    pallas_call x1, Pallas kernels: 51.8 us -> 54.9 us  [local(): pl.pallas_call(functools.partial(exchange, n, t), out_shape=(jax.ShapeDty...]
    pallas_call x1, Pallas kernels: 6.2 us -> 7.92 us  [local(): pl.pallas_call(weight_grads, grid=(n,), out_shape=(jax.ShapeDtypeStruct((...]
    unnamed x1 -> x0, other arithmetic: 1.35 us -> none
where the time goes in v1:
time: 63.7 us; the launch traced here: 63.4 us
  Pallas kernels  62.8 us (99%)
  between operations  0.64 us (1%)
    pallas_call x1, Pallas kernels, local(): pl.pallas_call(functools.partial(exchange, n, t), out_shape=(jax.ShapeDty...  54.9 us
    pallas_call x1, Pallas kernels, local(): pl.pallas_call(weight_grads, grid=(n,), out_shape=(jax.ShapeDtypeStruct((...  7.92 us

profile of v1, /device:TPU:1, one launch (start us, length us, event | category | flops | bytes accessed | tf_op | source)
XLA Modules:
  0.0 63.4 jit_solution(12048159766201698996)
XLA Ops:
  0.6 54.9 %exchange.1 = (bf16[2,512,128]{2,1,0:T(8,128)(2,1)}, bf16[8,2,128,256]{3,2,1,0:T(8,128)(2,1)}, f32[32,1024]{1,0:T(8,128)}) custom-call(bf16[1,32,2048]{2,1,0:T(8,128)(2,1)} %acts.1, bf16[1,512,1024]{2,1,0:T(8,128)(2,1)} %w_enc.1, f32[1,1024]{1,0:T(1,128)} %bias.1, bf16[1,8,1024,512]{3,2,1,0:T(8,128)(2,1)} %w_dec.1, bf16[1,128,512]{2,1,0:T(8,128)(2,1)} %targets.1), custom_call_target="tpu_custom_call" | custom-call | tf_op jit(solution)/shard_map/exchange/pallas_call | solution.py:424
  55.5 7.9 %weight_grads.1 = (bf16[1,8,1024,512]{3,2,1,0:T(8,128)(2,1)}, f32[32,1024]{1,0:T(8,128)}) custom-call(bf16[2,512,128]{2,1,0:T(8,128)(2,1)} %get-tuple-element.7.codes, bf16[8,2,128,256]{3,2,1,0:T(8,128)(2,1)} %get-tuple-element.8.errs, f32[32,1024]{1,0:T(8,128)} %get-tuple-element.9.grads_in), custom_call_target="tpu_custom_call" | custom-call | tf_op jit(solution)/shard_map/weight_grads/pallas_call | solution.py:464

commit v2 on v1

--- a/solution.py
+++ b/solution.py
@@ -33,7 +33,7 @@
     tokens = rows * t
     first = 2 * g
     count = n - first
-    whole = n - max(0, min(n // 2, n - 4))
+    whole = n - max(0, min(n // 4, n - 4))
 
     def remote(src, dst, send, recv, layer, tok):
         return pltpu.make_async_remote_copy(
@@ -166,8 +166,7 @@
     def share_lands(j):
         return ((j > first) | ((p == 0) & (g > 0))) & ((g > 0) | (j < whole))
 
-    def decode(q, _):
-        j = n - 1 - q
+    def decode(j):
         dec_copy(j).wait()
         both = []
         for h in range(2):
@@ -181,6 +180,10 @@
         held[j] = jnp.where(p == 0, both[0], both[1])
         mix_out[j] = jnp.where(p == 0, both[1], both[0]).astype(BF)
 
+        @pl.when(j + 4 < n)
+        def _():
+            mix(j + 4).wait_send()
+
         @pl.when(mix_leaves(j))
         def _():
             mix(j).start()
@@ -189,120 +192,107 @@
         def _():
             err_v[j, 1] = mix_out[j]
 
+
+    def gather_pair(j):
+        @pl.when(mix_lands(j))
+        def _():
+            mix(j).wait_recv()
+            held[j] = held[j] + mix_in[j].astype(F32)
+
+    def wait_ahead(j):
+        @pl.when(g > 0)
+        def _():
+            ahead(j).wait_recv()
+
+    def wait_back(j):
+        @pl.when(j >= first + 2)
+        def _():
+            back(j).wait_recv()
+
+    def send_ahead(j):
+        @pl.when(j >= first + 2)
+        def _():
+            fwd_out[j] = (held[j] + fwd_in[j].astype(F32)).astype(BF)
+            ahead(j).start()
+
+    def send_back(j):
+        @pl.when((g > 1) | ((g == 1) & (j < whole)))
+        def _():
+            bwd_out[j] = (held[j] + bwd_in[j].astype(F32)).astype(BF)
+            back(j).start()
+
+    def finish(j):
+        total = held[j] + fwd_in[j].astype(F32) + bwd_in[j].astype(F32)
+        err_v[j, p] = total.astype(BF)
+
+        @pl.when(share_leaves(j))
+        def _():
+            share(j).start()
+
+    def arrive(j):
+        @pl.when(share_lands(j))
+        def _():
+            share_land(j).wait_recv()
+
+        @pl.when((g == 0) & (j >= whole))
+        def _():
+            direct(j).wait_recv()
+
+        @pl.when((g == 1) & (j >= whole))
+        def _():
+            direct(j).start()
+
+    early = (g > 0) & (g < groups // 2)
+
+    lower = g < groups // 2
+    lag_one, lag_two, lag_three = 4, 7, 9
+
+    def step(q, _):
+        @pl.when(q < count)
+        def _():
+            decode(n - 1 - q)
+
+        @pl.when((q >= lag_one) & (q < count + lag_one))
+        def _():
+            j = n - 1 - q + lag_one
+            gather_pair(j)
+
+            @pl.when(lower)
+            def _():
+                wait_ahead(j)
+                send_ahead(j)
+
+            @pl.when(jnp.logical_not(lower))
+            def _():
+                wait_back(j)
+                send_back(j)
+
+        @pl.when((q >= lag_two) & (q < count + lag_two))
+        def _():
+            j = n - 1 - q + lag_two
+
+            @pl.when(lower & ((g > 0) | (j < whole)))
+            def _():
+                wait_back(j)
+                send_back(j)
+                finish(j)
+
+            @pl.when(jnp.logical_not(lower))
+            def _():
+                wait_ahead(j)
+                send_ahead(j)
+                finish(j)
+
+        @pl.when(early & (q >= lag_three))
+        def _():
+            arrive(n - 1 - q + lag_three)
+
         return 0
 
-    lax.fori_loop(0, count, decode, 0)
+    lax.fori_loop(0, count + lag_three, step, 0)
     for h in range(2):
         codes[h] = codes_v[h].T
     cg[...] = jnp.zeros_like(cg)
-
-    def gather_pair(j):
-        @pl.when(mix_lands(j))
-        def _():
-            mix(j).wait_recv()
-            held[j] = held[j] + mix_in[j].astype(F32)
-
-    def wait_ahead(j):
-        @pl.when(g > 0)
-        def _():
-            ahead(j).wait_recv()
-
-    def wait_back(j):
-        @pl.when(j >= first + 2)
-        def _():
-            back(j).wait_recv()
-
-    def send_ahead(j):
-        @pl.when(j >= first + 2)
-        def _():
-            fwd_out[j] = (held[j] + fwd_in[j].astype(F32)).astype(BF)
-            ahead(j).start()
-
-    def send_back(j):
-        @pl.when((g > 1) | ((g == 1) & (j < whole)))
-        def _():
-            bwd_out[j] = (held[j] + bwd_in[j].astype(F32)).astype(BF)
-            back(j).start()
-
-    def finish(j):
-        total = held[j] + fwd_in[j].astype(F32) + bwd_in[j].astype(F32)
-        err_v[j, p] = total.astype(BF)
-
-        @pl.when(share_leaves(j))
-        def _():
-            share(j).start()
-
-    def arrive(j):
-        @pl.when(share_lands(j))
-        def _():
-            share_land(j).wait_recv()
-
-        @pl.when((g == 0) & (j >= whole))
-        def _():
-            direct(j).wait_recv()
-
-        @pl.when((g == 1) & (j >= whole))
-        def _():
-            direct(j).start()
-
-    early = (g > 0) & (g < groups // 2)
-
-    @pl.when(g == 0)
-    def _():
-        def one(q, _):
-            j = n - 1 - q
-            gather_pair(j)
-            send_ahead(j)
-            return 0
-
-        def two(q, _):
-            j = whole - 1 - q
-            wait_back(j)
-            finish(j)
-            return 0
-
-        lax.fori_loop(0, n, one, 0)
-        lax.fori_loop(0, whole, two, 0)
-
-    @pl.when(early)
-    def _():
-        def one(q, _):
-            @pl.when(q < count)
-            def _():
-                j = n - 1 - q
-                gather_pair(j)
-                wait_ahead(j)
-                send_ahead(j)
-                wait_back(j)
-                send_back(j)
-                finish(j)
-
-            @pl.when(q >= 2)
-            def _():
-                arrive(n + 1 - q)
-
-            return 0
-
-        lax.fori_loop(0, count + 2, one, 0)
-
-    @pl.when((g > 0) & (g >= groups // 2))
-    def _():
-        def one(q, _):
-            j = n - 1 - q
-            gather_pair(j)
-            wait_back(j)
-            send_back(j)
-            return 0
-
-        def two(q, _):
-            j = n - 1 - q
-            wait_ahead(j)
-            send_ahead(j)
-            finish(j)
-            return 0
-
-        lax.fori_loop(0, count, one, 0)
-        lax.fori_loop(0, count, two, 0)
 
     def backward(q, _):
         j = n - 1 - q
@@ -374,7 +364,7 @@
     def drain(q, _):
         j = n - 1 - q
 
-        @pl.when(mix_leaves(j))
+        @pl.when(mix_leaves(j) & (j < first + 4))
         def _():
             mix(j).wait_send()
 
@@ -402,10 +392,11 @@
 def weight_grads(codes, errs, grads_in, dec, grads):
     grads[...] = grads_in[...]
     half_f, half_w = codes.shape[1], errs.shape[3]
-    for a in range(2):
-        for b in range(2):
-            dec[0, 0, a * half_f:(a + 1) * half_f, b * half_w:(b + 1) * half_w] = jnp.dot(
-                codes[a], errs[0, b], preferred_element_type=F32
+    for j in range(errs.shape[0]):
+        both = jnp.concatenate([errs[j, 0], errs[j, 1]], axis=1)
+        for a in range(2):
+            dec[0, j, a * half_f:(a + 1) * half_f, :] = jnp.dot(
+                codes[a], both, preferred_element_type=F32
             ).astype(BF)
 
 
@@ -463,18 +454,18 @@
     )(acts, w_enc, b_enc, w_dec, targets)
     dec, code_share = pl.pallas_call(
         weight_grads,
-        grid=(n,),
+        grid=(n // 2,),
         out_shape=(
             jax.ShapeDtypeStruct((1, n, features, width), BF),
             jax.ShapeDtypeStruct((rows, features), F32),
         ),
         in_specs=[
             pl.BlockSpec((2, half_f, tokens), lambda j: (0, 0, 0)),
-            pl.BlockSpec((1, 2, tokens, half_w), lambda j: (j, 0, 0, 0)),
+            pl.BlockSpec((2, 2, tokens, half_w), lambda j: (j, 0, 0, 0)),
             pl.BlockSpec((rows, features), lambda j: (0, 0)),
         ],
         out_specs=(
-            pl.BlockSpec((1, 1, features, width), lambda j: (0, j, 0, 0)),
+            pl.BlockSpec((1, 2, features, width), lambda j: (0, j, 0, 0)),
             pl.BlockSpec((rows, features), lambda j: (0, 0)),
         ),
         compiler_params=pltpu.CompilerParams(vmem_limit_bytes=58 * 2**20),

time: 63.7 us -> 60.5 us (0.950)
  Pallas kernels: 62.8 us -> 59.7 us
    pallas_call x1, Pallas kernels: 7.92 us -> 6.24 us  [local(): pl.pallas_call(weight_grads, grid=(n // 2,), out_shape=(jax.ShapeDtypeStr...]
    pallas_call x1, Pallas kernels: 54.9 us -> 53.5 us  [local(): pl.pallas_call(functools.partial(exchange, n, t), out_shape=(jax.ShapeDty...]
where the time goes in v2:
time: 60.5 us; the launch traced here: 60.4 us
  Pallas kernels  59.7 us (99%)
  between operations  0.64 us (1%)
    pallas_call x1, Pallas kernels, local(): pl.pallas_call(functools.partial(exchange, n, t), out_shape=(jax.ShapeDty...  53.5 us
    pallas_call x1, Pallas kernels, local(): pl.pallas_call(weight_grads, grid=(n // 2,), out_shape=(jax.ShapeDtypeStr...  6.24 us

profile of v2, /device:TPU:1, one launch (start us, length us, event | category | flops | bytes accessed | tf_op | source)
XLA Modules:
  0.0 60.4 jit_solution(809885677946298581)
XLA Ops:
  0.6 53.5 %exchange.1 = (bf16[2,512,128]{2,1,0:T(8,128)(2,1)}, bf16[8,2,128,256]{3,2,1,0:T(8,128)(2,1)}, f32[32,1024]{1,0:T(8,128)}) custom-call(bf16[1,32,2048]{2,1,0:T(8,128)(2,1)} %acts.1, bf16[1,512,1024]{2,1,0:T(8,128)(2,1)} %w_enc.1, f32[1,1024]{1,0:T(1,128)} %bias.1, bf16[1,8,1024,512]{3,2,1,0:T(8,128)(2,1)} %w_dec.1, bf16[1,128,512]{2,1,0:T(8,128)(2,1)} %targets.1), custom_call_target="tpu_custom_call" | custom-call | tf_op jit(solution)/shard_map/exchange/pallas_call | solution.py:415
  54.1 6.2 %weight_grads.1 = (bf16[1,8,1024,512]{3,2,1,0:T(8,128)(2,1)}, f32[32,1024]{1,0:T(8,128)}) custom-call(bf16[2,512,128]{2,1,0:T(8,128)(2,1)} %get-tuple-element.7.codes, bf16[8,2,128,256]{3,2,1,0:T(8,128)(2,1)} %get-tuple-element.8.errs, f32[32,1024]{1,0:T(8,128)} %get-tuple-element.9.grads_in), custom_call_target="tpu_custom_call" | custom-call | tf_op jit(solution)/shard_map/weight_grads/pallas_call | solution.py:455
